TPU v7x, 32 devices: a whole 2x2x4 slice. The times are simulated.
32 devices in a mesh: grp: 2 (over y), seq: 4 (over z), head: 4 (over x, core).
Axes of the slice: x: 2, y: 2, z: 4, core: 2. Of those that a mesh axis runs over, the one named last changes fastest.
Arguments:
- queries: bfloat16 [5120, 8192], P(('grp', 'seq'), 'head'), parts along dimension 0, may hold values from -6 to 6
- keys: bfloat16 [5120, 8192], P(('grp', 'seq'), 'head'), parts along dimension 0, may hold values from -6 to 6
- values: bfloat16 [5120, 8192], P(('grp', 'seq'), 'head'), parts along dimension 0, may hold values from -40 to 40, as said below
- gain: float32 [8192], P('head'), may hold values from 0.5 to 1.5
- head_order: int32 [128], P('grp'), parts along dimension 0, may hold values from 0 to 63, each once
Outputs:
- attended: bfloat16 [5120, 8192], P(('grp', 'seq'), 'head'), parts along dimension 0
- final_state: float32 [128, 128, 128], P(('grp', 'seq'), 'head'), parts along dimension 0
There are 2 independent parts, one for each index of `grp`. A program takes and returns all parts, laid end to end along the dimension named above; an argument that names none is the same for every part. Nothing has to cross between parts.
Inputs may be any that keep to these rules, and one draw needn't show every extreme that they name: `head_order`: each head appears exactly once. values of order one to some tens.
All inputs are finite; a program needn't handle non-finite values.
Results may differ from a plain program's by a relative error of at most 0.005.
Values sent between devices are 32-bit elements; how exact they have to be, the bound alone decides.
A program may use at most 128 MiB of HBM per device.

v0:
```python
import jax
import jax.numpy as jnp
from jax import lax
from jax.sharding import PartitionSpec as P

DH = 128


def prefix_2(part, axis, combine, identity):
    place = lax.axis_index(axis)
    gathered = lax.all_gather(part, axis)
    state = jnp.zeros_like(part) + jnp.asarray(identity, part.dtype)

    def one(turn, state):
        return combine(state, lax.dynamic_index_in_dim(gathered, turn, 0, False))

    return lax.fori_loop(0, place, one, state)


def add_states(earlier, later):
    return earlier + later


def on_device(queries, keys, values, gain, head_order):
    tok_rows = queries.shape[0]
    heads_here = queries.shape[1] // DH
    q_heads = queries.reshape(tok_rows, heads_here, DH)
    k_heads = keys.reshape(tok_rows, heads_here, DH)
    v_heads = values.reshape(tok_rows, heads_here, DH)
    local_state = jnp.einsum("thd,the->hde", k_heads, v_heads, preferred_element_type=jnp.float32)
    prefix = prefix_2(local_state, "seq", add_states, jnp.zeros_like(local_state))
    prefix_low = prefix.astype(jnp.bfloat16)
    causal = jnp.arange(tok_rows)[:, None] >= jnp.arange(tok_rows)[None, :]
    scores = jnp.einsum("thd,uhd->htu", q_heads, k_heads, preferred_element_type=jnp.float32)
    scores = jnp.where(causal[None], scores, 0.0).astype(jnp.bfloat16)
    mixed = jnp.einsum("htu,uhe->the", scores, v_heads, preferred_element_type=jnp.float32)
    mixed = mixed + jnp.einsum(
        "thd,hde->the", q_heads, prefix_low, preferred_element_type=jnp.float32
    )
    meansq = jnp.mean(mixed * mixed, axis=-1, keepdims=True)
    normed = mixed * lax.rsqrt(meansq + 1e-06) * gain.reshape(heads_here, DH)[None]
    attended = normed.astype(jnp.bfloat16).reshape(tok_rows, heads_here * DH)
    head_slices = lax.all_to_all(local_state, "head", split_axis=1, concat_axis=0, tiled=True)
    ordered = jnp.take(head_slices, head_order, axis=0)
    final_state = lax.psum_scatter(ordered, "seq", scatter_dimension=0, tiled=True)
    return (attended, final_state)


def solution(mesh):
    return jax.shard_map(
        on_device,
        mesh=mesh,
        in_specs=(
            P(("grp", "seq"), "head"),
            P(("grp", "seq"), "head"),
            P(("grp", "seq"), "head"),
            P("head"),
            P("grp"),
        ),
        out_specs=(P(("grp", "seq"), "head"), P(("grp", "seq"), "head", None)),
        check_vma=False,
    )
```

profile of v0, /device:TPU:0, one launch (start us, length us, event | category | flops | bytes accessed | tf_op | source)
XLA Modules:
  0.0 135.1 jit_solution(4203094108062880448)
XLA Ops:
  7.2 0.0 copy-start
  7.2 0.0 all-gather.3.cloned.1.call-start
  7.2 4.5 %copy.42 = bf16[640,2048]{0,1:T(8,128)(2,1)} copy(bf16[640,2048]{1,0:T(8,128)(2,1)} %param.8) | data formatting | bytes 5242880 | tf_op jit(solution)/shard_map/reshape | solution.py:28
  11.8 4.3 %fusion.2 = f32[16,128,128]{2,1,0:T(8,128)} fusion(bf16[640,16,128]{0,2,1:T(8,128)(2,1)} %bitcast.52, bf16[640,2048]{1,0:T(8,128)(2,1)} %param.9), kind=kOutput, calls=%fused_computation.8 | convolution fusion | flops 335544320 | bytes 6291456 | tf_op jit(solution)/shard_map/thd,the->hde/dot_general | solution.py:30
  16.1 0.0 copy-start.2
  16.1 0.0 all-gather.3.cloned.1.call-update
  16.1 2.8 %copy.36 = f32[16,128,128]{2,0,1:T(8,128)} copy(f32[16,128,128]{2,1,0:T(8,128)} %fusion.2) | data formatting | bytes 2097152 | tf_op jit(solution)/shard_map/thd,the->hde/dot_general | solution.py:30
  19.0 4.2 %all-to-all-start = ((f32[16,128,128]{2,0,1:T(8,128)}), f32[16,128,128]{2,0,1:T(8,128)}, u32[]{:S(2)}, u32[]{:S(2)}) async-start(f32[16,128,128]{2,0,1:T(8,128)} %copy.36), calls=%async_computation | async-start | bytes 2097152 | tf_op jit(solution)/shard_map/all_to_all | solution.py:43
  23.2 0.0 reduce-scatter.2.cloned.1.call-start
  23.3 0.0 copy-done.2
  23.3 0.1 iota_compare_fusion
  23.5 0.0 copy-done
  23.5 10.9 %fusion = f32[16,640,128]{1,2,0:T(8,128)} fusion(bf16[640,16,128]{0,2,1:T(8,128)(2,1)} %bitcast.53, pred[640,640]{1,0:T(8,128)(4,1)S(1)} %iota_compare_fusion, bf16[640,2048]{1,0:T(8,128)(2,1)} %param.9, bf16[640,2048]{1,0:T(8,128)(2,1)S(1)} %copy-done), kind=kOutput, calls=%fused_computation.6 | convolution fusion | flops 3368550400 | bytes 13516800 | tf_op jit(solution)/shard_map/htu,uhe->the/dot_general | solution.py:36
  34.3 4.0 %all-to-all-done = f32[16,128,128]{2,0,1:T(8,128)} async-done(((f32[16,128,128]{2,0,1:T(8,128)}), f32[16,128,128]{2,0,1:T(8,128)}, u32[]{:S(2)}, u32[]{:S(2)}) %all-to-all-start) | async-done | bytes 1048608 | tf_op jit(solution)/shard_map/all_to_all | solution.py:43
  38.3 2.5 %copy.38 = f32[4,16,32,128]{3,2,1,0:T(8,128)} copy(f32[4,16,32,128]{3,1,2,0:T(8,128)} %bitcast.8) | data formatting | bytes 2097152 | tf_op jit(solution)/shard_map/all_to_all | solution.py:43
  40.9 2.8 %gather_fusion = f32[64,32,128]{2,1,0:T(8,128)} fusion(f32[64,32,128]{2,1,0:T(8,128)} %bitcast.51, s32[1024]{0:T(1024)S(1)} %pad_clamp_fusion), kind=kCustom, calls=%fused_computation | custom fusion | bytes 2097408 | tf_op jit(solution)/shard_map/jit(_take)/gather | solution.py:44
  43.7 2.4 %broadcast_select_fusion = f32[64,32,128]{2,1,0:T(8,128)} fusion(f32[64,32,128]{2,1,0:T(8,128)} %gather_fusion, pred[64]{0:T(512)(128)(4,1)S(1)} %compare_and_fusion), kind=kLoop, calls=%fused_computation.18 | loop fusion | flops 262144 | bytes 2097216 | tf_op jit(solution)/shard_map/jit(_take)/select_n | solution.py:44
  46.1 0.0 reduce-scatter.2.cloned.1.call-update
  46.1 53.7 %all-gather.3.cloned.1.call-done = f32[64,128,128]{2,1,0:T(8,128)} async-done(((f32[16,128,128]{2,1,0:T(8,128)}), f32[64,128,128]{2,1,0:T(8,128)}) %all-gather.3.cloned.1.call-update) | async-done | bytes 4194320 | tf_op jit(solution)/shard_map/all_gather | solution.py:11
  99.7 1.1 broadcast_in_dim.33
  100.8 0.0 copy-start.1
  100.8 4.1 %multiply_reduce_fusion = (f32[640,16]{0,1:T(8,128)S(1)}, f32[640,16,128]{0,2,1:T(8,128)S(1)}) fusion(f32[16,128,128]{2,1,0:T(8,128)} %get-tuple-element.25, f32[16,640,128]{1,2,0:T(8,128)} %fusion, bf16[640,2048]{1,0:T(8,128)(2,1)S(1)} %copy-done), kind=kOutput, calls=%fused_computation.5 | convolution fusion | flops 339728384 | bytes 14196736 | tf_op jit(solution)/shard_map/thd,hde->the/dot_general | solution.py:37
  104.9 0.0 copy-done.1
  104.9 2.2 %multiply_convert_fusion = bf16[640,16,128]{0,2,1:T(8,128)(2,1)} fusion(f32[640,16,128]{0,2,1:T(8,128)S(1)} %get-tuple-element.43, f32[16,128]{1,0:T(8,128)S(1)} %bitcast.54, f32[640,16]{0,1:T(8,128)S(1)} %add_rsqrt_fusion), kind=kLoop, calls=%fused_computation.4 | loop fusion | flops 3932160 | bytes 7913472 | tf_op jit(solution)/shard_map/convert_element_type | solution.py:42
  107.2 4.4 %copy.39 = bf16[640,2048]{1,0:T(8,128)(2,1)} copy(bf16[640,2048]{0,1:T(8,128)(2,1)} %bitcast.49) | data formatting | bytes 5242880
  111.6 16.7 %reduce-scatter.2.cloned.1.call-done = f32[16,32,128]{2,1,0:T(8,128)} async-done(((f32[64,32,128]{2,1,0:T(8,128)}), f32[16,32,128]{2,1,0:T(8,128)}) %reduce-scatter.2.cloned.1.call-update) | async-done | bytes 262160 | tf_op jit(solution)/shard_map/reduce_scatter | solution.py:45
  (5 shorter events, 0.0 us)
Async XLA Ops:
  7.2 16.3 %copy-start = (bf16[640,2048]{1,0:T(8,128)(2,1)S(1)}, bf16[640,2048]{1,0:T(8,128)(2,1)}, u32[]{:S(2)}) copy-start(bf16[640,2048]{1,0:T(8,128)(2,1)} %param.7) | copy-start | bytes 7864324
  7.2 92.6 %all-gather.3.cloned.1.call-start = ((), (), s32[]{:S(2)}) async-start(), calls=%async_computation.3 | async-start | bytes 5242880 | tf_op jit(solution)/shard_map/all_gather | solution.py:11
  16.1 7.2 %copy-start.2 = (s32[64]{0:T(128)S(1)}, s32[64]{0:T(128)}, u32[]{:S(2)}) copy-start(s32[64]{0:T(128)} %param.11) | copy-start | bytes 772
  19.0 19.4 %all-to-all-start = ((f32[16,128,128]{2,0,1:T(8,128)}), f32[16,128,128]{2,0,1:T(8,128)}, u32[]{:S(2)}, u32[]{:S(2)}) async-start(f32[16,128,128]{2,0,1:T(8,128)} %copy.36), calls=%async_computation | async-start | bytes 2097152 | tf_op jit(solution)/shard_map/all_to_all | solution.py:43
  23.2 105.1 %reduce-scatter.2.cloned.1.call-start = ((), (), s32[]{:S(2)}) async-start(), calls=%async_computation.2 | async-start | bytes 1310720 | tf_op jit(solution)/shard_map/reduce_scatter | solution.py:45
  100.8 4.1 %copy-start.1 = (f32[2048]{0:T(1024)S(1)}, f32[2048]{0:T(1024)}, u32[]{:S(2)}) copy-start(f32[2048]{0:T(1024)} %param.10) | copy-start | bytes 24580
Sparse Core Ops, SparseCore 0:
  16.2 83.4 all-gather.2
  102.6 25.6 reduce-scatter.1
where the time goes:
time: 136 us; the launch traced here: 135 us
  waiting for transfers between devices  74.5 us (55%)
  matrix products  19.3 us (14%)
  local copies, waits for them, and re-layouts  18.2 us (13%)
  between operations  14.1 us (10%)
  other arithmetic  4.76 us (4%)
  starting transfers between devices  4.33 us (3%)
    all_gather x1, waiting for transfers between devices, prefix_2(): gathered = lax.all_gather(part, axis)  53.7 us
    reduce_scatter x1, waiting for transfers between devices, on_device(): lax.psum_scatter(ordered, 'seq', scatter_dimension=0, tiled=True)  16.7 us
    dot_general x1, matrix products, on_device(): jnp.einsum('htu,uhe->the', scores, v_heads, preferred_element_type=jnp.fl...  10.9 us
    reshape x1, local copies, waits for them, and re-layouts, on_device(): k_heads = keys.reshape(tok_rows, heads_here, DH)  4.53 us
    unnamed x7, local copies, waits for them, and re-layouts  4.4 us
    dot_general x1, matrix products, on_device(): jnp.einsum('thd,the->hde', k_heads, v_heads, preferred_element_type=jnp.f...  4.35 us
    all_to_all x1, starting transfers between devices, on_device(): lax.all_to_all(local_state, 'head', split_axis=1, concat_axis=0, tiled=True)  4.25 us
    dot_general x1, matrix products, on_device(): jnp.einsum('thd,hde->the', q_heads, prefix_low, preferred_element_type=jn...  4.06 us
  transfers between devices with their start and end apart: 3, of which 3 were waited for; matrix products, arithmetic and copies ran while one was open for 25% of the time, Pallas kernels for 0%

commit v1 on v0

v1 whole, which is shorter than its diff:
```python
import functools

import jax
import jax.numpy as jnp
from jax import lax
from jax.experimental import pallas as pl
from jax.experimental.pallas import tpu as pltpu
from jax.sharding import PartitionSpec as P

DH = 128
TILE = 256
EPS = 1e-06
MESH = pl.DeviceIdType.MESH


def dot(a, b, contract):
    return lax.dot_general(a, b, ((contract[:1], contract[1:]), ((), ())), preferred_element_type=jnp.float32)


def kernel(
    n_seq,
    n_head,
    q_hbm,
    k_hbm,
    v_hbm,
    gain_ref,
    order_ref,
    out_hbm,
    final_ref,
    q,
    k,
    v,
    mixed,
    att,
    block,
    up_in,
    up_out,
    down_in,
    down_out,
    total,
    rows,
    in_sem,
    out_sem,
    up_send,
    up_recv,
    down_send,
    down_recv,
    row_send,
    row_recv,
):
    heads, toks, _ = q.shape
    slots, part, _ = final_ref.shape
    s = lax.axis_index("seq")
    r = lax.axis_index("head")
    last = n_seq - 1
    upper = lax.rem(s + 1, n_seq)
    lower = lax.rem(s + last, n_seq)
    has_upper, has_lower = s < last, s > 0

    barrier = pltpu.get_barrier_semaphore()

    @pl.when(has_upper)
    def _():
        pl.semaphore_signal(barrier, inc=1, device_id={"seq": upper}, device_id_type=MESH)

    @pl.when(has_lower)
    def _():
        pl.semaphore_signal(barrier, inc=1, device_id={"seq": lower}, device_id_type=MESH)

    for d in range(1, n_head):
        pl.semaphore_signal(barrier, inc=1, device_id={"head": lax.rem(r + d, n_head)}, device_id_type=MESH)

    def load(i, h):
        hbm, vmem = ((k_hbm, k), (v_hbm, v), (q_hbm, q))[i]
        columns = pl.ds(pl.multiple_of(h * DH, DH), DH)
        return pltpu.make_async_copy(hbm.at[:, columns], vmem.at[h], in_sem.at[i, h])

    def store(h):
        columns = pl.ds(pl.multiple_of(h * DH, DH), DH)
        return pltpu.make_async_copy(att.at[h], out_hbm.at[:, columns], out_sem.at[h])

    def go_up(h):
        return pltpu.make_async_remote_copy(
            src_ref=up_out.at[h], dst_ref=up_in.at[h], send_sem=up_send.at[h], recv_sem=up_recv.at[h],
            device_id={"seq": upper}, device_id_type=MESH,
        )

    def go_down(h):
        return pltpu.make_async_remote_copy(
            src_ref=down_out.at[h], dst_ref=down_in.at[h], send_sem=down_send.at[h], recv_sem=down_recv.at[h],
            device_id={"seq": lower}, device_id_type=MESH,
        )

    def give_rows(d, h):
        peer = lax.rem(r + d, n_head)
        return pltpu.make_async_remote_copy(
            src_ref=total.at[h, pl.ds(pl.multiple_of(peer * part, part), part)],
            dst_ref=rows.at[r * heads + h],
            send_sem=row_send.at[d - 1, h], recv_sem=row_recv.at[d - 1, h],
            device_id={"head": peer}, device_id_type=MESH,
        )

    def start_loads(h, _):
        for i in range(3):
            load(i, h).start()
        return 0

    lax.fori_loop(0, heads, start_loads, 0)
    pl.semaphore_wait(barrier, n_head - 1 + has_upper.astype(jnp.int32) + has_lower.astype(jnp.int32))

    def step(t, _):
        @pl.when(t < heads)
        def _():
            load(0, t).wait()
            load(1, t).wait()
            block[t] = dot(k[t], v[t], (0, 0))

        c = t - s

        @pl.when((c >= 0) & (c < heads))
        def _():
            @pl.when(has_lower)
            def _():
                go_up(c).wait_recv()

            @pl.when(s == 0)
            def _():
                up_in[c] = jnp.zeros((DH, DH), jnp.float32)

            @pl.when(has_upper)
            def _():
                up_out[c] = up_in[c] + block[c]
                go_up(c).start()

        e = t - (last - s)

        @pl.when((e >= 0) & (e < heads))
        def _():
            @pl.when(has_upper)
            def _():
                go_down(e).wait_recv()

            @pl.when(s == last)
            def _():
                down_in[e] = jnp.zeros((DH, DH), jnp.float32)

            @pl.when(has_lower)
            def _():
                down_out[e] = down_in[e] + block[e]
                go_down(e).start()

        w = t - jnp.maximum(s, last - s)

        @pl.when((w >= 0) & (w < heads))
        def _():
            total[w] = up_in[w] + block[w] + down_in[w]
            for d in range(1, n_head):
                give_rows(d, w).start()
            rows[r * heads + w] = total[w, pl.ds(pl.multiple_of(r * part, part), part)]

        @pl.when(t < heads)
        def _():
            load(2, t).wait()
            for lo in range(0, toks, TILE):
                hi = min(lo + TILE, toks)
                q_rows = q[t, lo:hi]
                diag = dot(q_rows, k[t, lo:hi], (1, 1))
                row = lax.broadcasted_iota(jnp.int32, diag.shape, 0)
                col = lax.broadcasted_iota(jnp.int32, diag.shape, 1)
                diag = jnp.where(row >= col, diag, 0.0).astype(jnp.bfloat16)
                acc = dot(diag, v[t, lo:hi], (1, 0))
                if lo:
                    off = dot(q_rows, k[t, :lo], (1, 1)).astype(jnp.bfloat16)
                    acc = acc + dot(off, v[t, :lo], (1, 0))
                mixed[t, lo:hi] = acc

        @pl.when((c >= 0) & (c < heads))
        def _():
            prefix_low = up_in[c].astype(jnp.bfloat16)
            whole = mixed[c] + dot(q[c], prefix_low, (1, 0))
            meansq = jnp.mean(whole * whole, axis=-1, keepdims=True)
            gain = gain_ref[:, pl.ds(pl.multiple_of(c * DH, DH), DH)]
            att[c] = (whole * lax.rsqrt(meansq + EPS) * gain).astype(att.dtype)
            store(c).start()

        return 0

    lax.fori_loop(0, heads + last, step, 0)

    def arrive(h, _):
        for d in range(1, n_head):
            give_rows(d, h).wait_recv()
        return 0

    lax.fori_loop(0, heads, arrive, 0)

    def slot(j, _):
        final_ref[j] = rows[order_ref[s * slots + j]]
        return 0

    lax.fori_loop(0, slots, slot, 0)

    def finish(h, _):
        store(h).wait()

        @pl.when(has_upper)
        def _():
            go_up(h).wait_send()

        @pl.when(has_lower)
        def _():
            go_down(h).wait_send()

        for d in range(1, n_head):
            give_rows(d, h).wait_send()
        return 0

    lax.fori_loop(0, heads, finish, 0)


def on_device(n_seq, n_head, queries, keys, values, gain, head_order):
    toks, width = queries.shape
    heads = width // DH
    slots, part = head_order.shape[0] // n_seq, DH // n_head
    low = pltpu.VMEM((heads, toks, DH), jnp.bfloat16)
    state = pltpu.VMEM((heads, DH, DH), jnp.float32)
    sems = pltpu.SemaphoreType.DMA((heads,))
    peer_sems = pltpu.SemaphoreType.DMA((n_head - 1, heads))
    return pl.pallas_call(
        functools.partial(kernel, n_seq, n_head),
        out_shape=(
            jax.ShapeDtypeStruct((toks, width), jnp.bfloat16),
            jax.ShapeDtypeStruct((slots, part, DH), jnp.float32),
        ),
        in_specs=[pl.BlockSpec(memory_space=pl.ANY)] * 3
        + [pl.BlockSpec(memory_space=pltpu.VMEM), pl.BlockSpec(memory_space=pltpu.SMEM)],
        out_specs=(pl.BlockSpec(memory_space=pl.ANY), pl.BlockSpec(memory_space=pltpu.VMEM)),
        scratch_shapes=[
            low, low, low,
            pltpu.VMEM((heads, toks, DH), jnp.float32),
            low,
            state, state, state, state, state, state,
            pltpu.VMEM((heads * n_head, part, DH), jnp.float32),
            pltpu.SemaphoreType.DMA((3, heads)),
            sems, sems, sems, sems, sems,
            peer_sems, peer_sems,
        ],
        compiler_params=pltpu.CompilerParams(
            collective_id=0, has_side_effects=True, vmem_limit_bytes=48 * 2**20
        ),
        cost_estimate=pl.CostEstimate(
            flops=4 * toks * (toks + DH) * width, bytes_accessed=8 * toks * width, transcendentals=0
        ),
    )(queries, keys, values, gain.reshape(1, width), head_order)


def solution(mesh):
    return jax.shard_map(
        functools.partial(on_device, mesh.shape["seq"], mesh.shape["head"]),
        mesh=mesh,
        in_specs=(
            P(("grp", "seq"), "head"),
            P(("grp", "seq"), "head"),
            P(("grp", "seq"), "head"),
            P("head"),
            P("grp"),
        ),
        out_specs=(P(("grp", "seq"), "head"), P(("grp", "seq"), "head", None)),
        check_vma=False,
    )
```

time: 136 us -> 73 us (0.54)
  waiting for transfers between devices: 74.5 us -> 0 us
  Pallas kernels: 0 us -> 66.8 us
  matrix products: 19.3 us -> 0 us
  between operations: 14.1 us -> 0.65 us
  local copies, waits for them, and re-layouts: 18.2 us -> 5.28 us
  other arithmetic: 4.76 us -> 0 us
  starting transfers between devices: 4.33 us -> 0 us
    pallas_call x0 -> x1, Pallas kernels: none -> 66.8 us  [on_device(): pl.pallas_call(functools.partial(kernel, n_seq, n_head), out_shape=(jax.S...]
    all_gather x1 -> x0, waiting for transfers between devices: 53.7 us -> none  [prefix_2(): gathered = lax.all_gather(part, axis)]
    dot_general x3 -> x0, matrix products: 19.3 us -> none  [the longest x1 10.9 us: on_device(): jnp.einsum('htu,uhe->the', scores, v_heads, preferred_element_type=jnp.fl...]
    reduce_scatter x1 -> x0, waiting for transfers between devices: 16.7 us -> none  [on_device(): lax.psum_scatter(ordered, 'seq', scatter_dimension=0, tiled=True)]
    reshape x1 -> x0, local copies, waits for them, and re-layouts: 4.53 us -> none  [on_device(): k_heads = keys.reshape(tok_rows, heads_here, DH)]
    all_to_all x1 -> x0, starting transfers between devices: 4.25 us -> none  [on_device(): lax.all_to_all(local_state, 'head', split_axis=1, concat_axis=0, tiled=True)]
    all_to_all x1 -> x0, waiting for transfers between devices: 4.02 us -> none  [on_device(): lax.all_to_all(local_state, 'head', split_axis=1, concat_axis=0, tiled=True)]
    dot_general x1 -> x0, local copies, waits for them, and re-layouts: 2.83 us -> none  [on_device(): jnp.einsum('thd,the->hde', k_heads, v_heads, preferred_element_type=jnp.f...]
  transfers between devices with their start and end apart: 3 -> 0, of which waited for: 3 -> 0; matrix products, arithmetic and copies ran while one was open for 25% -> 0% of each run, Pallas kernels for 0% -> 0%
where the time goes in v1:
time: 73 us; the launch traced here: 72.8 us
  Pallas kernels  66.8 us (92%)
  local copies, waits for them, and re-layouts  5.28 us (7%)
    pallas_call x1, Pallas kernels, on_device(): pl.pallas_call(functools.partial(kernel, n_seq, n_head), out_shape=(jax.S...  66.8 us
    unnamed x8, local copies, waits for them, and re-layouts  5.28 us

profile of v1, /device:TPU:0, one launch (start us, length us, event | category | flops | bytes accessed | tf_op | source)
XLA Modules:
  0.0 72.8 jit_solution(9932783975772850691)
XLA Ops:
  0.6 0.0 copy-start
  0.6 1.7 %copy-done = bf16[640,2048]{1,0:T(8,128)(2,1)S(1)} copy-done((bf16[640,2048]{1,0:T(8,128)(2,1)S(1)}, bf16[640,2048]{1,0:T(8,128)(2,1)}, u32[]{:S(2)}) %copy-start) | copy-done | bytes 2621464
  2.4 0.0 copy-start.1
  2.4 0.7 copy-done.1
  3.1 0.0 copy-start.2
  3.1 0.7 copy-done.2
  3.7 66.8 %shard_map.68 = (bf16[640,2048]{1,0:T(8,128)(2,1)S(1)}, f32[16,32,128]{2,1,0:T(8,128)S(1)}) custom-call(bf16[640,2048]{1,0:T(8,128)(2,1)S(1)} %copy-done, bf16[640,2048]{1,0:T(8,128)(2,1)} %k_hbm.1, bf16[640,2048]{1,0:T(8,128)(2,1)} %v_hbm.1, f32[1,2048]{1,0:T(1,128)S(1)} %bitcast.1, s32[64]{0:T(128)S(1)} %copy-done.2), custom_call_target="tpu_custom_call" | custom-call | flops 4026531840 | bytes 10485760 | tf_op jit(solution)/shard_map/pallas_call | solution.py:229
  70.6 1.5 %copy.9 = bf16[640,2048]{1,0:T(8,128)(2,1)} copy(bf16[640,2048]{1,0:T(8,128)(2,1)S(1)} %get-tuple-element.4) | data formatting | bytes 5242880
  72.1 0.7 copy.10
Async XLA Ops:
  0.6 1.7 %copy-start = (bf16[640,2048]{1,0:T(8,128)(2,1)S(1)}, bf16[640,2048]{1,0:T(8,128)(2,1)}, u32[]{:S(2)}) copy-start(bf16[640,2048]{1,0:T(8,128)(2,1)} %q_hbm.1) | copy-start | bytes 7864324
  2.4 0.7 copy-start.1
  3.1 0.7 copy-start.2
